TPU v7x, 32 devices: a whole 2x2x4 slice. The times are simulated.
32 devices in a mesh: chain: 8 (over z, y), seg: 4 (over x, core).
Axes of the slice: x: 2, y: 2, z: 4, core: 2. Of those that a mesh axis runs over, the one named last changes fastest.
Arguments:
- band_tiles: bfloat16 [8, 1024, 7, 1024], P('chain', None, None, 'seg'), may hold values from -0.009765625 to 0.009765625
- widths: int32 [8], P('chain'), may hold values from 2 to 6, as said below
- warm_start: float32 [8192, 256], P(('chain', 'seg')), may hold values from -4 to 4
- scores: float32 [8192, 64], P(('chain', 'seg')), may hold values from -6 to 6
- penalty: float32 [256], replicated, may hold values from 0.05 to 0.5
Outputs:
- fitted_effects: float32 [8192, 256], P(('chain', 'seg'))
Inputs may be any that keep to these rules, and one draw needn't show every extreme that they name: `widths`: each block uses between 2 and 6 forward tiles; both 2 and 6 occur in every draw.
All inputs are finite; a program needn't handle non-finite values.
Results may differ from a plain program's by a relative error of at most 0.00085.
Values may be sent and summed in bfloat16 or wider, within the bound.
A program may use at most 64 MiB of HBM per device.

v0:
```python
import jax
import jax.numpy as jnp
from jax import lax
from jax.sharding import PartitionSpec as P

ITERS = 2


step_size = 0.8


def shifted(value, axis, by):
    length = lax.axis_size(axis)
    pairs = [(i, i + by) for i in range(length) if 0 <= i + by < length]
    return lax.ppermute(value, axis, pairs)


def soft_limit(values, limit):
    return jnp.sign(values) * jnp.maximum(jnp.abs(values) - limit, 0.0)


def per_device(band_tiles, widths, warm_start, scores, penalty):
    local_tiles = band_tiles[0]
    block_len = local_tiles.shape[0]
    depth = local_tiles.shape[1]
    strip_len = local_tiles.shape[2]
    flat_tiles = local_tiles.reshape(block_len, depth * strip_len)
    columns = warm_start.shape[1]
    path_len = columns // scores.shape[1]
    target = jnp.tile(scores, (1, path_len))
    offsets = jnp.arange(depth, dtype=jnp.int32)
    live_flags = offsets <= widths[0]
    live_half = live_flags.astype(jnp.bfloat16)
    live_full = live_flags.astype(jnp.float32)
    estimate = warm_start
    for iteration in range(ITERS):
        current = estimate.astype(jnp.bfloat16)
        whole_block = lax.all_gather(current, "seg", axis=0, tiled=True)
        ahead_list = [current] + [
            shifted(current, "chain", -shift_by) for shift_by in range(1, depth)
        ]
        stacked = (jnp.stack(ahead_list) * live_half[:, None, None]).reshape(
            depth * strip_len, columns
        )

        def forward_term(start_row, count, stacked=stacked):
            return jnp.dot(flat_tiles, stacked, preferred_element_type=jnp.float32)

        forward = lax.psum_scatter(
            forward_term(jnp.int32(0), strip_len * lax.axis_size("seg")).astype(jnp.bfloat16),
            "seg",
            scatter_dimension=0,
            tiled=True,
        ).astype(jnp.float32)
        outgoing = lax.dot_general(
            flat_tiles, whole_block, (((0,), (0,)), ((), ())), preferred_element_type=jnp.float32
        )
        outgoing = outgoing.reshape(depth, strip_len, columns) * live_full[:, None, None]
        backward = outgoing[0]
        for shift_by in range(1, depth):
            backward = backward + shifted(
                outgoing[shift_by].astype(jnp.bfloat16), "chain", shift_by
            ).astype(jnp.float32)
        stepped = estimate - step_size * (estimate + (forward + backward) - target)
        estimate = soft_limit(stepped, step_size * penalty)
    return estimate


def solution(mesh):
    in_specs = (
        P("chain", None, None, "seg"),
        P("chain"),
        P(("chain", "seg"), None),
        P(("chain", "seg"), None),
        P(),
    )
    out_specs = P(("chain", "seg"), None)
    return jax.shard_map(
        per_device, mesh=mesh, in_specs=in_specs, out_specs=out_specs, check_vma=False
    )
```

profile of v0, /device:TPU:20, one launch (start us, length us, event | category | flops | bytes accessed | tf_op | source)
XLA Modules:
  0.0 151.2 jit_solution(3930564888840236814)
XLA Ops:
  6.5 1.1 copy.18
  7.7 0.7 collective-permute-start.5
  8.3 1.4 collective-permute-start.4
  9.7 2.8 %collective-permute-start.3 = (bf16[256,256]{0,1:T(8,128)(2,1)S(1)}, bf16[256,256]{0,1:T(8,128)(2,1)S(1)}, u32[]{:S(2)}, u32[]{:S(2)}) collective-permute-start(bf16[256,256]{0,1:T(8,128)(2,1)S(1)} %get-tuple-element.10), channel_id=1, source_target_pairs={{16,0},{20,4},{24,8},{28,12},{17,1},{21,5},{25,9},{29,13},{18,2},{... | collective-permute-start | bytes 393224 | tf_op jit(solution)/shard_map/ppermute | solution.py:15
  12.5 1.3 collective-permute-start.2
  13.8 3.4 %collective-permute-start = (bf16[256,256]{0,1:T(8,128)(2,1)S(1)}, bf16[256,256]{0,1:T(8,128)(2,1)S(1)}, u32[]{:S(2)}, u32[]{:S(2)}) collective-permute-start(bf16[256,256]{0,1:T(8,128)(2,1)S(1)} %get-tuple-element.10), channel_id=1, source_target_pairs={{4,0},{8,4},{12,8},{16,12},{20,16},{24,20},{28,24},{5,1},{9,5},{13... | collective-permute-start | bytes 393224 | tf_op jit(solution)/shard_map/ppermute | solution.py:15
  17.2 7.2 %all_gather.6 = bf16[1024,256]{0,1:T(8,128)(2,1)S(1)} all-gather(bf16[256,256]{0,1:T(8,128)(2,1)S(1)} %get-tuple-element.10), channel_id=1, replica_groups=mesh['chain'=8,'seg'=4] {'seg'}, dimensions={0}, use_global_device_ids=true | all-gather | bytes 655360 | tf_op jit(solution)/shard_map/all_gather | solution.py:38
  25.0 6.1 %copy.14 = bf16[1,1024,7,256]{1,3,2,0:T(8,128)(2,1)} copy(bf16[1,1024,7,256]{3,1,2,0:T(8,128)(2,1)} %param.5) | data formatting | bytes 7340032 | tf_op args[0]
  31.1 3.1 %collective-permute-start.1 = (bf16[256,256]{0,1:T(8,128)(2,1)S(1)}, bf16[256,256]{0,1:T(8,128)(2,1)S(1)}, u32[]{:S(2)}, u32[]{:S(2)}) collective-permute-start(bf16[256,256]{0,1:T(8,128)(2,1)S(1)} %get-tuple-element.10), channel_id=1, source_target_pairs={{8,0},{12,4},{16,8},{20,12},{24,16},{28,20},{9,1},{13,5},{17,9},{2... | collective-permute-start | bytes 393224 | tf_op jit(solution)/shard_map/ppermute | solution.py:15
  34.2 4.6 %collective-permute-done.1 = bf16[256,256]{0,1:T(8,128)(2,1)S(1)} collective-permute-done((bf16[256,256]{0,1:T(8,128)(2,1)S(1)}, bf16[256,256]{0,1:T(8,128)(2,1)S(1)}, u32[]{:S(2)}, u32[]{:S(2)}) %collective-permute-start.1) | collective-permute-done | bytes 131104 | tf_op jit(solution)/shard_map/ppermute | solution.py:15
  39.6 4.0 %fusion.5 = bf16[1024,256]{0,1:T(8,128)(2,1)} fusion(bf16[1792,256]{1,0:T(8,128)(2,1)S(1)} %bitcast.149, bf16[1024,1792]{0,1:T(8,128)(2,1)} %bitcast.145), kind=kOutput, calls=%fused_computation.6 | convolution fusion | flops 939786240 | bytes 5111808 | tf_op jit(solution)/shard_map/dot_general | solution.py:47
  43.7 3.2 %fusion.29 = (bf16[7,256,256]{1,2,0:T(8,128)(2,1)S(1)}, f32[7,256,256]{1,2,0:T(8,128)S(1)}) fusion(f32[7]{0:T(128)S(1)} %compare_convert_fusion, bf16[1024,256]{0,1:T(8,128)(2,1)S(1)} %all_gather.6, bf16[1,1024,7,256]{1,3,2,0:T(8,128)(2,1)} %copy.14), kind=kOutput, calls=%fused_computation.68 | convolution fusion | flops 940441600 | bytes 6946844 | tf_op jit(solution)/shard_map/dot_general | solution.py:55
  47.0 1.9 %collective-permute-start.6 = (bf16[256,256]{0,1:T(8,128)(2,1)S(1)}, bf16[256,256]{0,1:T(8,128)(2,1)S(1)}, u32[]{:S(2)}, u32[]{:S(2)}) collective-permute-start(bf16[256,256]{0,1:T(8,128)(2,1)S(1)} %get-tuple-element.17), channel_id=1, source_target_pairs={{0,4},{4,8},{8,12},{12,16},{16,20},{20,24},{24,28},{1,5},{5,9},{9,... | collective-permute-start | bytes 393224 | tf_op jit(solution)/shard_map/ppermute | solution.py:15
  48.9 0.7 collective-permute-start.11
  49.6 1.3 collective-permute-start.10
  50.9 1.3 collective-permute-start.9
  52.2 1.3 collective-permute-start.8
  53.9 1.9 %collective-permute-start.7 = (bf16[256,256]{0,1:T(8,128)(2,1)S(1)}, bf16[256,256]{0,1:T(8,128)(2,1)S(1)}, u32[]{:S(2)}, u32[]{:S(2)}) collective-permute-start(bf16[256,256]{0,1:T(8,128)(2,1)S(1)} %get-tuple-element.22), channel_id=1, source_target_pairs={{0,8},{4,12},{8,16},{12,20},{16,24},{20,28},{1,9},{5,13},{9,17},{1... | collective-permute-start | bytes 393224 | tf_op jit(solution)/shard_map/ppermute | solution.py:15
  55.8 5.6 %collective-permute-done.10 = bf16[256,256]{0,1:T(8,128)(2,1)S(1)} collective-permute-done((bf16[256,256]{0,1:T(8,128)(2,1)S(1)}, bf16[256,256]{0,1:T(8,128)(2,1)S(1)}, u32[]{:S(2)}, u32[]{:S(2)}) %collective-permute-start.10) | collective-permute-done | bytes 131104 | tf_op jit(solution)/shard_map/ppermute | solution.py:15
  61.4 2.1 %collective-permute-done.9 = bf16[256,256]{0,1:T(8,128)(2,1)S(1)} collective-permute-done((bf16[256,256]{0,1:T(8,128)(2,1)S(1)}, bf16[256,256]{0,1:T(8,128)(2,1)S(1)}, u32[]{:S(2)}, u32[]{:S(2)}) %collective-permute-start.9) | collective-permute-done | bytes 131104 | tf_op jit(solution)/shard_map/ppermute | solution.py:15
  63.5 7.5 %collective-permute-done.8 = bf16[256,256]{0,1:T(8,128)(2,1)S(1)} collective-permute-done((bf16[256,256]{0,1:T(8,128)(2,1)S(1)}, bf16[256,256]{0,1:T(8,128)(2,1)S(1)}, u32[]{:S(2)}, u32[]{:S(2)}) %collective-permute-start.8) | collective-permute-done | bytes 131104 | tf_op jit(solution)/shard_map/ppermute | solution.py:15
  71.0 2.5 %collective-permute-done.7 = bf16[256,256]{0,1:T(8,128)(2,1)S(1)} collective-permute-done((bf16[256,256]{0,1:T(8,128)(2,1)S(1)}, bf16[256,256]{0,1:T(8,128)(2,1)S(1)}, u32[]{:S(2)}, u32[]{:S(2)}) %collective-permute-start.7) | collective-permute-done | bytes 131104 | tf_op jit(solution)/shard_map/ppermute | solution.py:15
  73.5 1.2 bitcast_dynamic-update-slice_fusion.6
  74.7 0.7 collective-permute-start.17
  75.4 1.3 collective-permute-start.16
  76.7 1.3 collective-permute-start.15
  78.0 1.3 collective-permute-start.14
  79.3 2.1 %collective-permute-start.12 = (bf16[256,256]{0,1:T(8,128)(2,1)S(1)}, bf16[256,256]{0,1:T(8,128)(2,1)S(1)}, u32[]{:S(2)}, u32[]{:S(2)}) collective-permute-start(bf16[256,256]{0,1:T(8,128)(2,1)S(1)} %get-tuple-element.6), channel_id=1, source_target_pairs={{4,0},{8,4},{12,8},{16,12},{20,16},{24,20},{28,24},{5,1},{9,5},{13... | collective-permute-start | bytes 393224 | tf_op jit(solution)/shard_map/ppermute | solution.py:15
  81.4 7.0 %all_gather.7 = bf16[1024,256]{0,1:T(8,128)(2,1)S(1)} all-gather(bf16[256,256]{0,1:T(8,128)(2,1)S(1)} %get-tuple-element.6), channel_id=1, replica_groups=mesh['chain'=8,'seg'=4] {'seg'}, dimensions={0}, use_global_device_ids=true | all-gather | bytes 655360 | tf_op jit(solution)/shard_map/all_gather | solution.py:38
  88.4 1.6 %collective-permute-done.12 = bf16[256,256]{0,1:T(8,128)(2,1)S(1)} collective-permute-done((bf16[256,256]{0,1:T(8,128)(2,1)S(1)}, bf16[256,256]{0,1:T(8,128)(2,1)S(1)}, u32[]{:S(2)}, u32[]{:S(2)}) %collective-permute-start.12) | collective-permute-done | bytes 131104 | tf_op jit(solution)/shard_map/ppermute | solution.py:15
  90.1 9.0 %collective-permute-start.13 = (bf16[256,256]{0,1:T(8,128)(2,1)S(1)}, bf16[256,256]{0,1:T(8,128)(2,1)S(1)}, u32[]{:S(2)}, u32[]{:S(2)}) collective-permute-start(bf16[256,256]{0,1:T(8,128)(2,1)S(1)} %get-tuple-element.6), channel_id=1, source_target_pairs={{8,0},{12,4},{16,8},{20,12},{24,16},{28,20},{9,1},{13,5},{17,9},{2... | collective-permute-start | bytes 393224 | tf_op jit(solution)/shard_map/ppermute | solution.py:15
  99.1 2.9 %collective-permute-done.13 = bf16[256,256]{0,1:T(8,128)(2,1)S(1)} collective-permute-done((bf16[256,256]{0,1:T(8,128)(2,1)S(1)}, bf16[256,256]{0,1:T(8,128)(2,1)S(1)}, u32[]{:S(2)}, u32[]{:S(2)}) %collective-permute-start.13) | collective-permute-done | bytes 131104 | tf_op jit(solution)/shard_map/ppermute | solution.py:15
  102.8 4.0 %fusion.6 = bf16[1024,256]{0,1:T(8,128)(2,1)} fusion(bf16[1792,256]{1,0:T(8,128)(2,1)S(1)} %bitcast.150, bf16[1024,1792]{0,1:T(8,128)(2,1)} %bitcast.146), kind=kOutput, calls=%fused_computation.7 | convolution fusion | flops 939786240 | bytes 5111808 | tf_op jit(solution)/shard_map/dot_general | solution.py:47
  106.8 3.2 %convolution_bitcast_fusion = f32[1792,256]{0,1:T(8,128)S(1)} fusion(bf16[1024,256]{0,1:T(8,128)(2,1)S(1)} %all_gather.7, bf16[1024,1792]{0,1:T(8,128)(2,1)} %bitcast.147), kind=kOutput, calls=%fused_computation.2 | convolution fusion | flops 939524096 | bytes 6029312 | tf_op jit(solution)/shard_map/dot_general | solution.py:55
  110.0 1.7 %copy.20 = f32[1792,256]{1,0:T(8,128)} copy(f32[1792,256]{0,1:T(8,128)S(1)} %convolution_bitcast_fusion) | data formatting | bytes 3670016 | tf_op jit(solution)/shard_map/dot_general | solution.py:55
  111.8 1.8 %copy.21 = f32[7,256,256]{1,2,0:T(8,128)S(1)} copy(f32[7,256,256]{2,1,0:T(8,128)} %bitcast.148) | data formatting | bytes 3670016 | tf_op jit(solution)/shard_map/reshape | solution.py:58
  113.6 1.6 %fusion.28 = (bf16[7,256,256]{1,2,0:T(8,128)(2,1)S(1)}, f32[7,256,256]{1,2,0:T(8,128)}) fusion(f32[7,256,256]{1,2,0:T(8,128)S(1)} %copy.21, f32[7]{0:T(128)S(1)} %compare_convert_fusion), kind=kLoop, calls=%fused_computation.67 | loop fusion | flops 917504 | bytes 4587548 | tf_op jit(solution)/shard_map/convert.5
  115.2 1.9 %collective-permute-start.18 = (bf16[256,256]{0,1:T(8,128)(2,1)S(1)}, bf16[256,256]{0,1:T(8,128)(2,1)S(1)}, u32[]{:S(2)}, u32[]{:S(2)}) collective-permute-start(bf16[256,256]{0,1:T(8,128)(2,1)S(1)} %get-tuple-element.11), channel_id=1, source_target_pairs={{0,4},{4,8},{8,12},{12,16},{16,20},{20,24},{24,28},{1,5},{5,9},{9,... | collective-permute-start | bytes 393224 | tf_op jit(solution)/shard_map/ppermute | solution.py:15
  117.8 1.3 collective-permute-start.22
  119.1 1.3 collective-permute-start.21
  120.4 1.3 collective-permute-start.20
  122.0 1.9 %collective-permute-start.19 = (bf16[256,256]{0,1:T(8,128)(2,1)S(1)}, bf16[256,256]{0,1:T(8,128)(2,1)S(1)}, u32[]{:S(2)}, u32[]{:S(2)}) collective-permute-start(bf16[256,256]{0,1:T(8,128)(2,1)S(1)} %get-tuple-element.16), channel_id=1, source_target_pairs={{0,8},{4,12},{8,16},{12,20},{16,24},{20,28},{1,9},{5,13},{9,17},{1... | collective-permute-start | bytes 393224 | tf_op jit(solution)/shard_map/ppermute | solution.py:15
  124.0 5.4 %collective-permute-done.22 = bf16[256,256]{0,1:T(8,128)(2,1)S(1)} collective-permute-done((bf16[256,256]{0,1:T(8,128)(2,1)S(1)}, bf16[256,256]{0,1:T(8,128)(2,1)S(1)}, u32[]{:S(2)}, u32[]{:S(2)}) %collective-permute-start.22) | collective-permute-done | bytes 131104 | tf_op jit(solution)/shard_map/ppermute | solution.py:15
  129.3 2.9 %collective-permute-done.21 = bf16[256,256]{0,1:T(8,128)(2,1)S(1)} collective-permute-done((bf16[256,256]{0,1:T(8,128)(2,1)S(1)}, bf16[256,256]{0,1:T(8,128)(2,1)S(1)}, u32[]{:S(2)}, u32[]{:S(2)}) %collective-permute-start.21) | collective-permute-done | bytes 131104 | tf_op jit(solution)/shard_map/ppermute | solution.py:15
  132.3 6.8 %collective-permute-done.20 = bf16[256,256]{0,1:T(8,128)(2,1)S(1)} collective-permute-done((bf16[256,256]{0,1:T(8,128)(2,1)S(1)}, bf16[256,256]{0,1:T(8,128)(2,1)S(1)}, u32[]{:S(2)}, u32[]{:S(2)}) %collective-permute-start.20) | collective-permute-done | bytes 131104 | tf_op jit(solution)/shard_map/ppermute | solution.py:15
  139.1 3.2 %collective-permute-done.19 = bf16[256,256]{0,1:T(8,128)(2,1)S(1)} collective-permute-done((bf16[256,256]{0,1:T(8,128)(2,1)S(1)}, bf16[256,256]{0,1:T(8,128)(2,1)S(1)}, u32[]{:S(2)}, u32[]{:S(2)}) %collective-permute-start.19) | collective-permute-done | bytes 131104 | tf_op jit(solution)/shard_map/ppermute | solution.py:15
  142.2 1.2 maximum_multiply_fusion
  143.5 0.8 copy.22
  (46 shorter events, 3.3 us)
Async XLA Ops:
  6.5 67.0 %reduce-scatter.3.cloned.1.call-start = ((), (), s32[]{:S(2)}) async-start(), calls=%async_computation.2 | async-start | bytes 655360 | tf_op jit(solution)/shard_map/reduce_scatter | solution.py:49
  7.7 31.2 %collective-permute-start.5 = (bf16[256,256]{0,1:T(8,128)(2,1)S(1)}, bf16[256,256]{0,1:T(8,128)(2,1)S(1)}, u32[]{:S(2)}, u32[]{:S(2)}) collective-permute-start(bf16[256,256]{0,1:T(8,128)(2,1)S(1)} %get-tuple-element.10), channel_id=1, source_target_pairs={{24,0},{28,4},{25,1},{29,5},{26,2},{30,6},{27,3},{31,7}} | collective-permute-start | bytes 393224 | tf_op jit(solution)/shard_map/ppermute | solution.py:15
  8.3 30.5 %collective-permute-start.4 = (bf16[256,256]{0,1:T(8,128)(2,1)S(1)}, bf16[256,256]{0,1:T(8,128)(2,1)S(1)}, u32[]{:S(2)}, u32[]{:S(2)}) collective-permute-start(bf16[256,256]{0,1:T(8,128)(2,1)S(1)} %get-tuple-element.10), channel_id=1, source_target_pairs={{20,0},{24,4},{28,8},{21,1},{25,5},{29,9},{22,2},{26,6},{30,10},{2... | collective-permute-start | bytes 393224 | tf_op jit(solution)/shard_map/ppermute | solution.py:15
  9.7 29.1 %collective-permute-start.3 = (bf16[256,256]{0,1:T(8,128)(2,1)S(1)}, bf16[256,256]{0,1:T(8,128)(2,1)S(1)}, u32[]{:S(2)}, u32[]{:S(2)}) collective-permute-start(bf16[256,256]{0,1:T(8,128)(2,1)S(1)} %get-tuple-element.10), channel_id=1, source_target_pairs={{16,0},{20,4},{24,8},{28,12},{17,1},{21,5},{25,9},{29,13},{18,2},{... | collective-permute-start | bytes 393224 | tf_op jit(solution)/shard_map/ppermute | solution.py:15
  12.5 26.2 %collective-permute-start.2 = (bf16[256,256]{0,1:T(8,128)(2,1)S(1)}, bf16[256,256]{0,1:T(8,128)(2,1)S(1)}, u32[]{:S(2)}, u32[]{:S(2)}) collective-permute-start(bf16[256,256]{0,1:T(8,128)(2,1)S(1)} %get-tuple-element.10), channel_id=1, source_target_pairs={{12,0},{16,4},{20,8},{24,12},{28,16},{13,1},{17,5},{21,9},{25,13},... | collective-permute-start | bytes 393224 | tf_op jit(solution)/shard_map/ppermute | solution.py:15
  13.8 17.3 %collective-permute-start = (bf16[256,256]{0,1:T(8,128)(2,1)S(1)}, bf16[256,256]{0,1:T(8,128)(2,1)S(1)}, u32[]{:S(2)}, u32[]{:S(2)}) collective-permute-start(bf16[256,256]{0,1:T(8,128)(2,1)S(1)} %get-tuple-element.10), channel_id=1, source_target_pairs={{4,0},{8,4},{12,8},{16,12},{20,16},{24,20},{28,24},{5,1},{9,5},{13... | collective-permute-start | bytes 393224 | tf_op jit(solution)/shard_map/ppermute | solution.py:15
  31.1 7.6 %collective-permute-start.1 = (bf16[256,256]{0,1:T(8,128)(2,1)S(1)}, bf16[256,256]{0,1:T(8,128)(2,1)S(1)}, u32[]{:S(2)}, u32[]{:S(2)}) collective-permute-start(bf16[256,256]{0,1:T(8,128)(2,1)S(1)} %get-tuple-element.10), channel_id=1, source_target_pairs={{8,0},{12,4},{16,8},{20,12},{24,16},{28,20},{9,1},{13,5},{17,9},{2... | collective-permute-start | bytes 393224 | tf_op jit(solution)/shard_map/ppermute | solution.py:15
  43.6 98.6 %reduce-scatter.5.cloned.1.call-start = ((), (), s32[]{:S(2)}) async-start(), calls=%async_computation.3 | async-start | bytes 655360 | tf_op jit(solution)/shard_map/reduce_scatter | solution.py:49
  43.7 12.1 %copy-start.1 = (f32[256]{0:T(256)S(1)}, f32[256]{0:T(256)}, u32[]{:S(2)}) copy-start(f32[256]{0:T(256)} %param.9) | copy-start | bytes 3076
  43.7 29.8 %copy-start = (f32[256,64]{0,1:T(8,128)S(1)}, f32[256,64]{0,1:T(8,128)}, u32[]{:S(2)}) copy-start(f32[256,64]{0,1:T(8,128)} %param.8) | copy-start | bytes 196612
  47.0 6.9 %collective-permute-start.6 = (bf16[256,256]{0,1:T(8,128)(2,1)S(1)}, bf16[256,256]{0,1:T(8,128)(2,1)S(1)}, u32[]{:S(2)}, u32[]{:S(2)}) collective-permute-start(bf16[256,256]{0,1:T(8,128)(2,1)S(1)} %get-tuple-element.17), channel_id=1, source_target_pairs={{0,4},{4,8},{8,12},{12,16},{16,20},{20,24},{24,28},{1,5},{5,9},{9,... | collective-permute-start | bytes 393224 | tf_op jit(solution)/shard_map/ppermute | solution.py:15
  48.9 6.9 %collective-permute-start.11 = (bf16[256,256]{0,1:T(8,128)(2,1)S(1)}, bf16[256,256]{0,1:T(8,128)(2,1)S(1)}, u32[]{:S(2)}, u32[]{:S(2)}) collective-permute-start(bf16[256,256]{0,1:T(8,128)(2,1)S(1)} %get-tuple-element.18), channel_id=1, source_target_pairs={{0,24},{4,28},{1,25},{5,29},{2,26},{6,30},{3,27},{7,31}} | collective-permute-start | bytes 393224 | tf_op jit(solution)/shard_map/ppermute | solution.py:15
  49.6 11.8 %collective-permute-start.10 = (bf16[256,256]{0,1:T(8,128)(2,1)S(1)}, bf16[256,256]{0,1:T(8,128)(2,1)S(1)}, u32[]{:S(2)}, u32[]{:S(2)}) collective-permute-start(bf16[256,256]{0,1:T(8,128)(2,1)S(1)} %get-tuple-element.19), channel_id=1, source_target_pairs={{0,20},{4,24},{8,28},{1,21},{5,25},{9,29},{2,22},{6,26},{10,30},{3... | collective-permute-start | bytes 393224 | tf_op jit(solution)/shard_map/ppermute | solution.py:15
  50.9 12.6 %collective-permute-start.9 = (bf16[256,256]{0,1:T(8,128)(2,1)S(1)}, bf16[256,256]{0,1:T(8,128)(2,1)S(1)}, u32[]{:S(2)}, u32[]{:S(2)}) collective-permute-start(bf16[256,256]{0,1:T(8,128)(2,1)S(1)} %get-tuple-element.20), channel_id=1, source_target_pairs={{0,16},{4,20},{8,24},{12,28},{1,17},{5,21},{9,25},{13,29},{2,18},{... | collective-permute-start | bytes 393224 | tf_op jit(solution)/shard_map/ppermute | solution.py:15
  52.2 18.8 %collective-permute-start.8 = (bf16[256,256]{0,1:T(8,128)(2,1)S(1)}, bf16[256,256]{0,1:T(8,128)(2,1)S(1)}, u32[]{:S(2)}, u32[]{:S(2)}) collective-permute-start(bf16[256,256]{0,1:T(8,128)(2,1)S(1)} %get-tuple-element.21), channel_id=1, source_target_pairs={{0,12},{4,16},{8,20},{12,24},{16,28},{1,13},{5,17},{9,21},{13,25},... | collective-permute-start | bytes 393224 | tf_op jit(solution)/shard_map/ppermute | solution.py:15
  53.9 19.6 %collective-permute-start.7 = (bf16[256,256]{0,1:T(8,128)(2,1)S(1)}, bf16[256,256]{0,1:T(8,128)(2,1)S(1)}, u32[]{:S(2)}, u32[]{:S(2)}) collective-permute-start(bf16[256,256]{0,1:T(8,128)(2,1)S(1)} %get-tuple-element.22), channel_id=1, source_target_pairs={{0,8},{4,12},{8,16},{12,20},{16,24},{20,28},{1,9},{5,13},{9,17},{1... | collective-permute-start | bytes 393224 | tf_op jit(solution)/shard_map/ppermute | solution.py:15
  74.7 27.4 %collective-permute-start.17 = (bf16[256,256]{0,1:T(8,128)(2,1)S(1)}, bf16[256,256]{0,1:T(8,128)(2,1)S(1)}, u32[]{:S(2)}, u32[]{:S(2)}) collective-permute-start(bf16[256,256]{0,1:T(8,128)(2,1)S(1)} %get-tuple-element.6), channel_id=1, source_target_pairs={{24,0},{28,4},{25,1},{29,5},{26,2},{30,6},{27,3},{31,7}} | collective-permute-start | bytes 393224 | tf_op jit(solution)/shard_map/ppermute | solution.py:15
  75.4 26.7 %collective-permute-start.16 = (bf16[256,256]{0,1:T(8,128)(2,1)S(1)}, bf16[256,256]{0,1:T(8,128)(2,1)S(1)}, u32[]{:S(2)}, u32[]{:S(2)}) collective-permute-start(bf16[256,256]{0,1:T(8,128)(2,1)S(1)} %get-tuple-element.6), channel_id=1, source_target_pairs={{20,0},{24,4},{28,8},{21,1},{25,5},{29,9},{22,2},{26,6},{30,10},{2... | collective-permute-start | bytes 393224 | tf_op jit(solution)/shard_map/ppermute | solution.py:15
  76.7 25.3 %collective-permute-start.15 = (bf16[256,256]{0,1:T(8,128)(2,1)S(1)}, bf16[256,256]{0,1:T(8,128)(2,1)S(1)}, u32[]{:S(2)}, u32[]{:S(2)}) collective-permute-start(bf16[256,256]{0,1:T(8,128)(2,1)S(1)} %get-tuple-element.6), channel_id=1, source_target_pairs={{16,0},{20,4},{24,8},{28,12},{17,1},{21,5},{25,9},{29,13},{18,2},{... | collective-permute-start | bytes 393224 | tf_op jit(solution)/shard_map/ppermute | solution.py:15
  78.0 24.0 %collective-permute-start.14 = (bf16[256,256]{0,1:T(8,128)(2,1)S(1)}, bf16[256,256]{0,1:T(8,128)(2,1)S(1)}, u32[]{:S(2)}, u32[]{:S(2)}) collective-permute-start(bf16[256,256]{0,1:T(8,128)(2,1)S(1)} %get-tuple-element.6), channel_id=1, source_target_pairs={{12,0},{16,4},{20,8},{24,12},{28,16},{13,1},{17,5},{21,9},{25,13},... | collective-permute-start | bytes 393224 | tf_op jit(solution)/shard_map/ppermute | solution.py:15
  79.3 10.8 %collective-permute-start.12 = (bf16[256,256]{0,1:T(8,128)(2,1)S(1)}, bf16[256,256]{0,1:T(8,128)(2,1)S(1)}, u32[]{:S(2)}, u32[]{:S(2)}) collective-permute-start(bf16[256,256]{0,1:T(8,128)(2,1)S(1)} %get-tuple-element.6), channel_id=1, source_target_pairs={{4,0},{8,4},{12,8},{16,12},{20,16},{24,20},{28,24},{5,1},{9,5},{13... | collective-permute-start | bytes 393224 | tf_op jit(solution)/shard_map/ppermute | solution.py:15
  90.1 11.9 %collective-permute-start.13 = (bf16[256,256]{0,1:T(8,128)(2,1)S(1)}, bf16[256,256]{0,1:T(8,128)(2,1)S(1)}, u32[]{:S(2)}, u32[]{:S(2)}) collective-permute-start(bf16[256,256]{0,1:T(8,128)(2,1)S(1)} %get-tuple-element.6), channel_id=1, source_target_pairs={{8,0},{12,4},{16,8},{20,12},{24,16},{28,20},{9,1},{13,5},{17,9},{2... | collective-permute-start | bytes 393224 | tf_op jit(solution)/shard_map/ppermute | solution.py:15
  115.2 6.9 %collective-permute-start.18 = (bf16[256,256]{0,1:T(8,128)(2,1)S(1)}, bf16[256,256]{0,1:T(8,128)(2,1)S(1)}, u32[]{:S(2)}, u32[]{:S(2)}) collective-permute-start(bf16[256,256]{0,1:T(8,128)(2,1)S(1)} %get-tuple-element.11), channel_id=1, source_target_pairs={{0,4},{4,8},{8,12},{12,16},{16,20},{20,24},{24,28},{1,5},{5,9},{9,... | collective-permute-start | bytes 393224 | tf_op jit(solution)/shard_map/ppermute | solution.py:15
  117.1 6.9 %collective-permute-start.23 = (bf16[256,256]{0,1:T(8,128)(2,1)S(1)}, bf16[256,256]{0,1:T(8,128)(2,1)S(1)}, u32[]{:S(2)}, u32[]{:S(2)}) collective-permute-start(bf16[256,256]{0,1:T(8,128)(2,1)S(1)} %get-tuple-element.12), channel_id=1, source_target_pairs={{0,24},{4,28},{1,25},{5,29},{2,26},{6,30},{3,27},{7,31}} | collective-permute-start | bytes 393224 | tf_op jit(solution)/shard_map/ppermute | solution.py:15
  117.8 11.5 %collective-permute-start.22 = (bf16[256,256]{0,1:T(8,128)(2,1)S(1)}, bf16[256,256]{0,1:T(8,128)(2,1)S(1)}, u32[]{:S(2)}, u32[]{:S(2)}) collective-permute-start(bf16[256,256]{0,1:T(8,128)(2,1)S(1)} %get-tuple-element.13), channel_id=1, source_target_pairs={{0,20},{4,24},{8,28},{1,21},{5,25},{9,29},{2,22},{6,26},{10,30},{3... | collective-permute-start | bytes 393224 | tf_op jit(solution)/shard_map/ppermute | solution.py:15
  119.1 13.2 %collective-permute-start.21 = (bf16[256,256]{0,1:T(8,128)(2,1)S(1)}, bf16[256,256]{0,1:T(8,128)(2,1)S(1)}, u32[]{:S(2)}, u32[]{:S(2)}) collective-permute-start(bf16[256,256]{0,1:T(8,128)(2,1)S(1)} %get-tuple-element.14), channel_id=1, source_target_pairs={{0,16},{4,20},{8,24},{12,28},{1,17},{5,21},{9,25},{13,29},{2,18},{... | collective-permute-start | bytes 393224 | tf_op jit(solution)/shard_map/ppermute | solution.py:15
  120.4 18.7 %collective-permute-start.20 = (bf16[256,256]{0,1:T(8,128)(2,1)S(1)}, bf16[256,256]{0,1:T(8,128)(2,1)S(1)}, u32[]{:S(2)}, u32[]{:S(2)}) collective-permute-start(bf16[256,256]{0,1:T(8,128)(2,1)S(1)} %get-tuple-element.15), channel_id=1, source_target_pairs={{0,12},{4,16},{8,20},{12,24},{16,28},{1,13},{5,17},{9,21},{13,25},... | collective-permute-start | bytes 393224 | tf_op jit(solution)/shard_map/ppermute | solution.py:15
  122.0 20.2 %collective-permute-start.19 = (bf16[256,256]{0,1:T(8,128)(2,1)S(1)}, bf16[256,256]{0,1:T(8,128)(2,1)S(1)}, u32[]{:S(2)}, u32[]{:S(2)}) collective-permute-start(bf16[256,256]{0,1:T(8,128)(2,1)S(1)} %get-tuple-element.16), channel_id=1, source_target_pairs={{0,8},{4,12},{8,16},{12,20},{16,24},{20,28},{1,9},{5,13},{9,17},{1... | collective-permute-start | bytes 393224 | tf_op jit(solution)/shard_map/ppermute | solution.py:15
Sparse Core Ops, SparseCore 0:
  43.7 21.5 reduce-scatter.2
  107.0 22.0 reduce-scatter.4
where the time goes:
time: 152 us; the launch traced here: 151 us
  waiting for transfers between devices  45.8 us (30%)
  starting transfers between devices  45 us (30%)
  between operations  14.5 us (10%)
  matrix products  14.4 us (9%)
  blocking collectives  14.2 us (9%)
  local copies, waits for them, and re-layouts  13 us (9%)
  other arithmetic  4.26 us (3%)
    ppermute x24, waiting for transfers between devices, shifted(): return lax.ppermute(value, axis, pairs)  45.8 us
    ppermute x24, starting transfers between devices, shifted(): return lax.ppermute(value, axis, pairs)  45 us
    all_gather x2, blocking collectives, per_device(): whole_block = lax.all_gather(current, 'seg', axis=0, tiled=True)  14.2 us
    dot_general x2, matrix products, forward_term(): return jnp.dot(flat_tiles, stacked, preferred_element_type=jnp.float32)  7.95 us
    unnamed x16, local copies, waits for them, and re-layouts  7.27 us
    dot_general x2, matrix products, per_device(): lax.dot_general(flat_tiles, whole_block, (((0,), (0,)), ((), ())), prefer...  6.42 us
  transfers between devices with their start and end apart: 26, of which 13 were waited for; matrix products, arithmetic and copies ran while one was open for 12% of the time, Pallas kernels for 0%

commit v1 on v0

v1 whole, which is shorter than its diff:
```python
import functools

import jax
import jax.numpy as jnp
from jax import lax
from jax.experimental import pallas as pl
from jax.experimental.pallas import tpu as pltpu
from jax.sharding import PartitionSpec as P

ITERS = 2
step_size = 0.8
F32 = jnp.float32
BF16 = jnp.bfloat16


def kernel(
    nchain, nseg, depth,
    tiles_hbm, widths, warm, scores_t, penalty, out,
    tiles, est, target, cur, cur_t, ag, even, odd, acc, rs_send, rs_recv,
    b_send, b_recv, y_send, y_recv, q_send, q_recv,
    tile_sem, ag_s, ag_r, ev_s, ev_r, od_s, od_r, ev_y, rs_s, rs_r, b_s, b_r, y_s, y_r, q_s, q_r,
):
    far = (depth - 1) // 2
    pairs = nchain // 2
    chain, seg = lax.axis_index("chain"), lax.axis_index("seg")
    p, y = chain // 2, chain % 2
    strip = cur.shape[1]
    partner = {"chain": 2 * p + 1 - y, "seg": seg}
    below = {"chain": chain - 2, "seg": seg}
    above = {"chain": chain + 2, "seg": seg}
    has_below, has_above = p >= 1, p + 1 < pairs

    def peer(o):
        return {"chain": chain, "seg": lax.rem(seg + o, nseg)}

    def loads(j):
        return pltpu.make_async_copy(tiles_hbm.at[j], tiles.at[j], tile_sem.at[j])

    for j in range(depth):
        loads(j).start()

    barrier = pltpu.get_barrier_semaphore()

    def greet(device):
        pl.semaphore_signal(barrier, inc=1, device_id=device, device_id_type=pl.DeviceIdType.MESH)

    for o in range(1, nseg):
        greet(peer(o))
    greet(partner)
    pl.when(has_below)(lambda: greet(below))
    pl.when(has_above)(lambda: greet(above))

    est[...] = warm[...]
    zero = jnp.zeros((strip, cur.shape[2]), BF16)
    for it in range(ITERS):
        for d in range(1, far + 1):
            @pl.when(p + d >= pairs)
            def _():
                even[it, d] = zero
                odd[it, d] = zero
        for d in range(far):
            @pl.when(p == 0)
            def _():
                b_recv[it, d, 0] = zero

            @pl.when((p == 0) | ((y == 0) if d == far - 1 else (p == 0)))
            def _():
                b_recv[it, d, 1] = zero

        @pl.when(y == 0)
        def _():
            q_recv[it] = zero

    limit = step_size * penalty[...]
    width = widths[0]

    def live(j):
        return jnp.where(j <= width, 1.0, 0.0).astype(F32)

    def send(src, dst, s_sem, r_sem, device):
        return pltpu.make_async_remote_copy(
            src_ref=src, dst_ref=dst, send_sem=s_sem, recv_sem=r_sem,
            device_id=device, device_id_type=pl.DeviceIdType.MESH,
        )

    pl.semaphore_wait(barrier, nseg + has_below.astype(jnp.int32) + has_above.astype(jnp.int32))

    def iteration(it, carry):
        def ag_copy(o):
            return send(cur_t.at[it], ag.at[it, o - 1], ag_s.at[it, o - 1], ag_r.at[it, o - 1], peer(o))

        def even_copy(d):
            src = cur.at[it] if d == 0 else even.at[it, d]
            return send(src, even.at[it, d + 1], ev_s.at[it, d], ev_r.at[it, d], below)

        def odd_copy(d):
            return send(odd.at[it, d], odd.at[it, d + 1], od_s.at[it, d], od_r.at[it, d], below)

        def cross_copy(d):
            src = cur.at[it] if d == 0 else even.at[it, d]
            return send(src, odd.at[it, d], ev_y.at[it, 0, d], ev_y.at[it, 1, d], partner)

        def up_copy(d, r):
            return send(
                b_send.at[it, d - 1, r], b_recv.at[it, d - 1, r], b_s.at[it, d - 1, r], b_r.at[it, d - 1, r], above
            )

        def y_copy():
            return send(y_send.at[it], y_recv.at[it], y_s.at[it], y_r.at[it], partner)

        def q_copy():
            return send(q_send.at[it], q_recv.at[it], q_s.at[it], q_r.at[it], partner)

        def rs_copy(o):
            return send(rs_send.at[it, o - 1], rs_recv.at[it, o - 1], rs_s.at[it, o - 1], rs_r.at[it, o - 1], peer(o))

        now = est[...]
        cur[it] = now.astype(BF16)
        pl.when(has_below)(lambda: even_copy(0).start())
        pl.when(y == 1)(lambda: cross_copy(0).start())
        cur_t[it] = now.T.astype(BF16)
        for o in range(1, nseg):
            ag_copy(o).start()

        @pl.when(it == 0)
        def _():
            path = cur.shape[2] // scores_t.shape[0]
            target[...] = jnp.concatenate([scores_t[...]] * path, axis=0).T
            for j in range(depth):
                loads(j).wait()

        @pl.when(has_above)
        def _():
            even_copy(0).wait_recv()
            pl.when(has_below)(lambda: even_copy(1).start())
            cross_copy(1).start()

        for o in range(1, nseg):
            ag_copy(o).wait_recv()

        def product(j):
            total = jnp.dot(
                cur_t[it], tiles[j, pl.ds(pl.multiple_of(seg * strip, strip), strip), :], preferred_element_type=F32
            )
            for o in range(1, nseg):
                owner = lax.rem(seg - o + nseg, nseg)
                rows = pl.ds(pl.multiple_of(owner * strip, strip), strip)
                total = total + jnp.dot(ag[it, o - 1], tiles[j, rows, :], preferred_element_type=F32)
            return total * live(j)

        @pl.when(p + far < pairs)
        def _():
            b_send[it, far - 1, 0] = product(2 * far).astype(BF16)
            up_copy(far, 0).start()

            @pl.when(y == 1)
            def _():
                b_send[it, far - 1, 1] = product(2 * far - 1).astype(BF16)
                up_copy(far, 1).start()

        @pl.when(has_above)
        def _():
            cross_copy(1).wait_recv()
            pl.when(has_below)(lambda: odd_copy(1).start())

        def relay_even(d):
            @pl.when(p + d < pairs)
            def _():
                even_copy(d - 1).wait_recv()
                if d < far:
                    pl.when(has_below)(lambda: even_copy(d).start())

        def relay_odd(d):
            def go():
                odd_copy(d - 1).wait_recv()
                if d < far:
                    pl.when(has_below & ((y == 1) | (d + 1 < far)))(lambda: odd_copy(d).start())

            pl.when((p + d < pairs) & ((y == 1) | (d < far)))(go)

        @pl.when(y == 0)
        def _():
            q_send[it] = product(1).astype(BF16)
            q_copy().start()

        for d in range(far - 1, 1, -1):
            relay_even(far + 1 - d)

            @pl.when(p + d < pairs)
            def _():
                value = product(2 * d)
                pl.when(has_below)(lambda: up_copy(d + 1, 0).wait_recv())
                b_send[it, d - 1, 0] = (value + b_recv[it, d, 0].astype(F32)).astype(BF16)
                up_copy(d, 0).start()
                value = product(2 * d + 1 - 2 * y)
                pl.when(has_below & ((y == 1) | (d + 1 < far)))(lambda: up_copy(d + 1, 1).wait_recv())
                b_send[it, d - 1, 1] = (value + b_recv[it, d, 1].astype(F32)).astype(BF16)
                up_copy(d, 1).start()

            relay_odd(far + 1 - d)

        @pl.when(has_above)
        def _():
            value = product(3 - 2 * y)
            pl.when(has_below)(lambda: up_copy(2, 1).wait_recv())
            y_send[it] = (value + b_recv[it, 1, 1].astype(F32)).astype(BF16)
            y_copy().start()

        pl.when(y == 0)(lambda: cross_copy(0).wait_recv())

        def term(rows, j):
            if j == 0:
                held = cur[it]
            elif j % 2 == 0:
                held = even[it, j // 2]
            else:
                held = odd[it, j // 2 + y]
            return jnp.dot(tiles[j, rows, :], held * live(j).astype(BF16), preferred_element_type=F32)

        for q in range(nseg):
            rows = pl.ds(q * strip, strip)
            total = term(rows, 0)
            for j in range(1, 2 * far - 1):
                total = total + term(rows, j)
            acc[rows, :] = total

        @pl.when(has_above)
        def _():
            value = product(2)
            pl.when(has_below)(lambda: up_copy(2, 0).wait_recv())
            y_copy().wait_recv()
            value = value + b_recv[it, 1, 0].astype(F32) + y_recv[it].astype(F32)
            b_send[it, 0, 0] = value.astype(BF16)
            up_copy(1, 0).start()

        relay_even(far)
        relay_odd(far)

        def rest(q):
            rows = pl.ds(pl.multiple_of(q * strip, strip), strip)
            total = acc[rows, :]
            for j in range(2 * far - 1, depth):
                total = total + term(rows, j)
            return total

        for o in range(1, nseg):
            rs_send[it, o - 1] = rest(lax.rem(seg + o, nseg)).astype(BF16)
            rs_copy(o).start()
        forward = rest(seg)
        back = product(0)
        pl.when(has_below)(lambda: up_copy(1, 0).wait_recv())
        pl.when(y == 1)(lambda: q_copy().wait_recv())
        back = back + b_recv[it, 0, 0].astype(F32) + q_recv[it].astype(F32)
        coupled = forward + back.T
        for o in range(1, nseg):
            rs_copy(o).wait_recv()
            coupled = coupled + rs_recv[it, o - 1].astype(F32)
        now = est[...]
        stepped = now - step_size * (now + coupled - target[...])
        est[...] = jnp.where(
            stepped > limit, stepped - limit, jnp.where(stepped < -limit, stepped + limit, 0.0)
        )

        for o in range(1, nseg):
            ag_copy(o).wait_send()
            rs_copy(o).wait_send()

        @pl.when(has_below)
        def _():
            even_copy(0).wait_send()
            for d in range(1, far):
                pl.when(p + d < pairs)(lambda: even_copy(d).wait_send())
                pl.when((p + d < pairs) & ((y == 1) | (d + 1 < far)))(lambda: odd_copy(d).wait_send())

        pl.when(y == 1)(lambda: cross_copy(0).wait_send())
        pl.when(y == 0)(lambda: q_copy().wait_send())

        @pl.when(has_above)
        def _():
            cross_copy(1).wait_send()
            y_copy().wait_send()
            up_copy(1, 0).wait_send()

        for d in range(2, far + 1):
            pl.when(p + d < pairs)(lambda: up_copy(d, 0).wait_send())
            pl.when((p + d < pairs) & ((y == 1) | (d < far)))(lambda: up_copy(d, 1).wait_send())
        return carry

    lax.fori_loop(0, ITERS, iteration, 0)
    out[...] = est[...]


def per_device(nchain, nseg, band_tiles, widths, warm_start, scores, penalty):
    tiles = jnp.transpose(band_tiles[0], (1, 0, 2))
    depth, block, strip = tiles.shape
    far = (depth - 1) // 2
    columns = warm_start.shape[1]
    one = (strip, columns)
    vmem = pl.BlockSpec(memory_space=pltpu.VMEM)
    dma = pltpu.SemaphoreType.DMA
    n = ITERS

    def buf(*lead, dtype=BF16):
        return pltpu.VMEM(lead + one, dtype)

    return pl.pallas_call(
        functools.partial(kernel, nchain, nseg, depth),
        out_shape=jax.ShapeDtypeStruct(one, F32),
        in_specs=[
            pl.BlockSpec(memory_space=pl.ANY), pl.BlockSpec(memory_space=pltpu.SMEM), vmem, vmem, vmem,
        ],
        out_specs=vmem,
        scratch_shapes=[
            pltpu.VMEM((depth, block, strip), BF16),
            buf(dtype=F32), buf(dtype=F32),
            buf(n), pltpu.VMEM((n, columns, strip), BF16), pltpu.VMEM((n, nseg - 1, columns, strip), BF16),
            buf(n, far + 1), buf(n, far + 1),
            pltpu.VMEM((block, columns), F32),
            buf(n, nseg - 1), buf(n, nseg - 1),
            buf(n, far, 2), buf(n, far, 2), buf(n), buf(n), buf(n), buf(n),
            dma((depth,)),
            dma((n, nseg)), dma((n, nseg)),
            dma((n, far)), dma((n, far)), dma((n, far)), dma((n, far)), dma((n, 2, 2)),
            dma((n, nseg)), dma((n, nseg)),
            dma((n, far, 2)), dma((n, far, 2)),
            dma((n,)), dma((n,)), dma((n,)), dma((n,)),
        ],
        compiler_params=pltpu.CompilerParams(
            collective_id=0, has_side_effects=True, vmem_limit_bytes=40 * 1024 * 1024
        ),
    )(tiles, widths, warm_start, scores.T, penalty[None, :])


def solution(mesh):
    in_specs = (
        P("chain", None, None, "seg"),
        P("chain"),
        P(("chain", "seg"), None),
        P(("chain", "seg"), None),
        P(),
    )
    out_specs = P(("chain", "seg"), None)
    return jax.shard_map(
        functools.partial(per_device, mesh.shape["chain"], mesh.shape["seg"]),
        mesh=mesh, in_specs=in_specs, out_specs=out_specs, check_vma=False,
    )
```

time: 152 us -> 68.6 us (0.45)
  the two profiles are of different devices: /device:TPU:20 before, /device:TPU:9 now
where the time goes in v1:
time: 68.6 us; the launch traced here: 68.3 us
  Pallas kernels  62.4 us (91%)
  local copies, waits for them, and re-layouts  5.2 us (8%)
    pallas_call x1, Pallas kernels, per_device(): pl.pallas_call(functools.partial(kernel, nchain, nseg, depth), out_shape=...  62.4 us
    unnamed x9, local copies, waits for them, and re-layouts  5.2 us

profile of v1, /device:TPU:9, one launch (start us, length us, event | category | flops | bytes accessed | tf_op | source)
XLA Modules:
  0.0 68.3 jit_solution(4312268327515507278)
XLA Ops:
  0.7 0.0 copy-start
  0.7 2.0 %copy-done = bf16[1,1024,7,256]{3,1,2,0:T(8,128)(2,1)S(1)} copy-done((bf16[1,1024,7,256]{3,1,2,0:T(8,128)(2,1)S(1)}, bf16[1,1024,7,256]{3,1,2,0:T(8,128)(2,1)}, u32[]{:S(2)}) %copy-start) | copy-done | bytes 3670040
  2.7 0.0 copy-start.1
  2.7 0.9 %copy-done.1 = f32[256,256]{1,0:T(8,128)S(1)} copy-done((f32[256,256]{1,0:T(8,128)S(1)}, f32[256,256]{1,0:T(8,128)}, u32[]{:S(2)}) %copy-start.1) | copy-done | bytes 262168
  3.6 0.0 copy-start.2
  3.6 0.8 %copy-done.2 = f32[256,64]{0,1:T(8,128)S(1)} copy-done((f32[256,64]{0,1:T(8,128)S(1)}, f32[256,64]{0,1:T(8,128)}, u32[]{:S(2)}) %copy-start.2) | copy-done | bytes 65560
  4.5 0.0 copy-start.3
  4.5 0.7 copy-done.3
  5.2 62.4 %shard_map.55 = f32[256,256]{1,0:T(8,128)S(1)} custom-call(bf16[7,1024,256]{2,1,0:T(8,128)(2,1)S(1)} %bitcast.5, s32[1]{0:T(128)S(6)} %copy.7.widths, f32[256,256]{1,0:T(8,128)S(1)} %copy-done.1, f32[64,256]{1,0:T(8,128)S(1)} %bitcast.6, f32[1,256]{1,0:T(1,128)S(1)} %bitcast.7), custom_call_target="tpu_custom_call" | custom-call | tf_op jit(solution)/shard_map/pallas_call | solution.py:306
  67.6 0.7 %copy.8 = f32[256,256]{1,0:T(8,128)} copy(f32[256,256]{1,0:T(8,128)S(1)} %shard_map.55) | data formatting | bytes 524288
Async XLA Ops:
  0.7 2.0 %copy-start = (bf16[1,1024,7,256]{3,1,2,0:T(8,128)(2,1)S(1)}, bf16[1,1024,7,256]{3,1,2,0:T(8,128)(2,1)}, u32[]{:S(2)}) copy-start(bf16[1,1024,7,256]{3,1,2,0:T(8,128)(2,1)} %param.5) | copy-start | bytes 11010052
  2.7 0.9 %copy-start.1 = (f32[256,256]{1,0:T(8,128)S(1)}, f32[256,256]{1,0:T(8,128)}, u32[]{:S(2)}) copy-start(f32[256,256]{1,0:T(8,128)} %warm.1) | copy-start | bytes 786436
  3.6 0.8 %copy-start.2 = (f32[256,64]{0,1:T(8,128)S(1)}, f32[256,64]{0,1:T(8,128)}, u32[]{:S(2)}) copy-start(f32[256,64]{0,1:T(8,128)} %param.8) | copy-start | bytes 196612
  4.5 0.7 copy-start.3

commit v2 on v1

--- a/solution.py
+++ b/solution.py
@@ -8,6 +8,7 @@
 from jax.sharding import PartitionSpec as P
 
 ITERS = 2
+GROUPS = 2
 step_size = 0.8
 F32 = jnp.float32
 BF16 = jnp.bfloat16
@@ -15,10 +16,10 @@
 
 def kernel(
     nchain, nseg, depth,
-    tiles_hbm, widths, warm, scores_t, penalty, out,
-    tiles, est, target, cur, cur_t, ag, even, odd, acc, rs_send, rs_recv,
+    tiles_hbm, widths, warm, scores_hbm, penalty_hbm, out,
+    tiles, est, scores_t, penalty, target, cur, cur_t, ag, even, odd, acc, rs_send, rs_recv,
     b_send, b_recv, y_send, y_recv, q_send, q_recv,
-    tile_sem, ag_s, ag_r, ev_s, ev_r, od_s, od_r, ev_y, rs_s, rs_r, b_s, b_r, y_s, y_r, q_s, q_r,
+    tile_sem, in_sem, ag_s, ag_r, ev_s, ev_r, od_s, od_r, ev_y, rs_s, rs_r, b_s, b_r, y_s, y_r, q_s, q_r,
 ):
     far = (depth - 1) // 2
     pairs = nchain // 2
@@ -36,6 +37,12 @@
     def loads(j):
         return pltpu.make_async_copy(tiles_hbm.at[j], tiles.at[j], tile_sem.at[j])
 
+    inputs = [
+        pltpu.make_async_copy(src, dst, in_sem.at[i])
+        for i, (src, dst) in enumerate(((warm, est), (penalty_hbm, penalty), (scores_hbm, scores_t)))
+    ]
+    for load in inputs:
+        load.start()
     for j in range(depth):
         loads(j).start()
 
@@ -50,9 +57,10 @@
     pl.when(has_below)(lambda: greet(below))
     pl.when(has_above)(lambda: greet(above))
 
-    est[...] = warm[...]
-    zero = jnp.zeros((strip, cur.shape[2]), BF16)
-    for it in range(ITERS):
+    wide = cur.shape[2]
+    zero = jnp.zeros((strip, wide), BF16)
+    zero_t = jnp.zeros((wide, strip), BF16)
+    for it in range(ITERS * GROUPS):
         for d in range(1, far + 1):
             @pl.when(p + d >= pairs)
             def _():
@@ -61,17 +69,16 @@
         for d in range(far):
             @pl.when(p == 0)
             def _():
-                b_recv[it, d, 0] = zero
+                b_recv[it, d, 0] = zero_t
 
             @pl.when((p == 0) | ((y == 0) if d == far - 1 else (p == 0)))
             def _():
-                b_recv[it, d, 1] = zero
+                b_recv[it, d, 1] = zero_t
 
         @pl.when(y == 0)
         def _():
-            q_recv[it] = zero
-
-    limit = step_size * penalty[...]
+            q_recv[it] = zero_t
+
     width = widths[0]
 
     def live(j):
@@ -85,7 +92,7 @@
 
     pl.semaphore_wait(barrier, nseg + has_below.astype(jnp.int32) + has_above.astype(jnp.int32))
 
-    def iteration(it, carry):
+    def transfers(it):
         def ag_copy(o):
             return send(cur_t.at[it], ag.at[it, o - 1], ag_s.at[it, o - 1], ag_r.at[it, o - 1], peer(o))
 
@@ -114,7 +121,11 @@
         def rs_copy(o):
             return send(rs_send.at[it, o - 1], rs_recv.at[it, o - 1], rs_s.at[it, o - 1], rs_r.at[it, o - 1], peer(o))
 
-        now = est[...]
+        return ag_copy, even_copy, odd_copy, cross_copy, up_copy, y_copy, q_copy, rs_copy
+
+    def iteration(it, columns, first, whole):
+        ag_copy, even_copy, odd_copy, cross_copy, up_copy, y_copy, q_copy, rs_copy = transfers(it)
+        now = est[:, columns]
         cur[it] = now.astype(BF16)
         pl.when(has_below)(lambda: even_copy(0).start())
         pl.when(y == 1)(lambda: cross_copy(0).start())
@@ -122,9 +133,11 @@
         for o in range(1, nseg):
             ag_copy(o).start()
 
-        @pl.when(it == 0)
-        def _():
-            path = cur.shape[2] // scores_t.shape[0]
+        yield
+        if first:
+            inputs[1].wait()
+            inputs[2].wait()
+            path = whole // scores_t.shape[0]
             target[...] = jnp.concatenate([scores_t[...]] * path, axis=0).T
             for j in range(depth):
                 loads(j).wait()
@@ -158,6 +171,8 @@
                 b_send[it, far - 1, 1] = product(2 * far - 1).astype(BF16)
                 up_copy(far, 1).start()
 
+        yield
+
         @pl.when(has_above)
         def _():
             cross_copy(1).wait_recv()
@@ -184,6 +199,7 @@
             q_copy().start()
 
         for d in range(far - 1, 1, -1):
+            yield
             relay_even(far + 1 - d)
 
             @pl.when(p + d < pairs)
@@ -199,6 +215,8 @@
 
             relay_odd(far + 1 - d)
 
+        yield
+
         @pl.when(has_above)
         def _():
             value = product(3 - 2 * y)
@@ -222,7 +240,9 @@
             total = term(rows, 0)
             for j in range(1, 2 * far - 1):
                 total = total + term(rows, j)
-            acc[rows, :] = total
+            acc[rows, columns] = total
+
+        yield
 
         @pl.when(has_above)
         def _():
@@ -235,10 +255,11 @@
 
         relay_even(far)
         relay_odd(far)
+        yield
 
         def rest(q):
             rows = pl.ds(pl.multiple_of(q * strip, strip), strip)
-            total = acc[rows, :]
+            total = acc[rows, columns]
             for j in range(2 * far - 1, depth):
                 total = total + term(rows, j)
             return total
@@ -247,6 +268,7 @@
             rs_send[it, o - 1] = rest(lax.rem(seg + o, nseg)).astype(BF16)
             rs_copy(o).start()
         forward = rest(seg)
+        yield
         back = product(0)
         pl.when(has_below)(lambda: up_copy(1, 0).wait_recv())
         pl.when(y == 1)(lambda: q_copy().wait_recv())
@@ -255,12 +277,26 @@
         for o in range(1, nseg):
             rs_copy(o).wait_recv()
             coupled = coupled + rs_recv[it, o - 1].astype(F32)
-        now = est[...]
-        stepped = now - step_size * (now + coupled - target[...])
-        est[...] = jnp.where(
+        now = est[:, columns]
+        limit = step_size * penalty[:, columns]
+        stepped = now - step_size * (now + coupled - target[:, columns])
+        est[:, columns] = jnp.where(
             stepped > limit, stepped - limit, jnp.where(stepped < -limit, stepped + limit, 0.0)
         )
 
+    inputs[0].wait()
+
+    def group(g):
+        for i in range(ITERS):
+            yield from iteration(i * GROUPS + g, slice(g * wide, (g + 1) * wide), i + g == 0, GROUPS * wide)
+
+    running = [group(g) for g in range(GROUPS)]
+    while running:
+        running = [one for one in running if next(one, running) is not running]
+    out[...] = est[...]
+
+    def drain(it, carry):
+        ag_copy, even_copy, odd_copy, cross_copy, up_copy, y_copy, q_copy, rs_copy = transfers(it)
         for o in range(1, nseg):
             ag_copy(o).wait_send()
             rs_copy(o).wait_send()
@@ -286,8 +322,7 @@
             pl.when((p + d < pairs) & ((y == 1) | (d < far)))(lambda: up_copy(d, 1).wait_send())
         return carry
 
-    lax.fori_loop(0, ITERS, iteration, 0)
-    out[...] = est[...]
+    lax.fori_loop(0, ITERS * GROUPS, drain, 0)
 
 
 def per_device(nchain, nseg, band_tiles, widths, warm_start, scores, penalty):
@@ -295,30 +330,34 @@
     depth, block, strip = tiles.shape
     far = (depth - 1) // 2
     columns = warm_start.shape[1]
-    one = (strip, columns)
-    vmem = pl.BlockSpec(memory_space=pltpu.VMEM)
+    wide = columns // GROUPS
+    hbm = pl.BlockSpec(memory_space=pltpu.HBM)
     dma = pltpu.SemaphoreType.DMA
-    n = ITERS
-
-    def buf(*lead, dtype=BF16):
-        return pltpu.VMEM(lead + one, dtype)
+    n = ITERS * GROUPS
+
+    def buf(*lead):
+        return pltpu.VMEM(lead + (strip, wide), BF16)
+
+    def turned(*lead):
+        return pltpu.VMEM(lead + (wide, strip), BF16)
 
     return pl.pallas_call(
         functools.partial(kernel, nchain, nseg, depth),
-        out_shape=jax.ShapeDtypeStruct(one, F32),
+        out_shape=jax.ShapeDtypeStruct((strip, columns), F32),
         in_specs=[
-            pl.BlockSpec(memory_space=pl.ANY), pl.BlockSpec(memory_space=pltpu.SMEM), vmem, vmem, vmem,
+            hbm, pl.BlockSpec(memory_space=pltpu.SMEM), hbm, hbm, hbm,
         ],
-        out_specs=vmem,
+        out_specs=pl.BlockSpec(memory_space=pltpu.VMEM),
         scratch_shapes=[
             pltpu.VMEM((depth, block, strip), BF16),
-            buf(dtype=F32), buf(dtype=F32),
-            buf(n), pltpu.VMEM((n, columns, strip), BF16), pltpu.VMEM((n, nseg - 1, columns, strip), BF16),
+            pltpu.VMEM((strip, columns), F32), pltpu.VMEM(scores.shape[::-1], F32), pltpu.VMEM((1, columns), F32),
+            pltpu.VMEM((strip, columns), F32),
+            buf(n), turned(n), turned(n, nseg - 1),
             buf(n, far + 1), buf(n, far + 1),
             pltpu.VMEM((block, columns), F32),
             buf(n, nseg - 1), buf(n, nseg - 1),
-            buf(n, far, 2), buf(n, far, 2), buf(n), buf(n), buf(n), buf(n),
-            dma((depth,)),
+            turned(n, far, 2), turned(n, far, 2), turned(n), turned(n), turned(n), turned(n),
+            dma((depth,)), dma((3,)),
             dma((n, nseg)), dma((n, nseg)),
             dma((n, far)), dma((n, far)), dma((n, far)), dma((n, far)), dma((n, 2, 2)),
             dma((n, nseg)), dma((n, nseg)),
@@ -326,7 +365,7 @@
             dma((n,)), dma((n,)), dma((n,)), dma((n,)),
         ],
         compiler_params=pltpu.CompilerParams(
-            collective_id=0, has_side_effects=True, vmem_limit_bytes=40 * 1024 * 1024
+            collective_id=0, has_side_effects=True, vmem_limit_bytes=63 * 1024 * 1024
         ),
     )(tiles, widths, warm_start, scores.T, penalty[None, :])
 

time: 68.6 us -> 60.3 us (0.88)
  Pallas kernels: 62.4 us -> 57.4 us
  local copies, waits for them, and re-layouts: 5.2 us -> 1.67 us
    pallas_call x1, Pallas kernels: 62.4 us -> 57.4 us  [per_device(): pl.pallas_call(functools.partial(kernel, nchain, nseg, depth), out_shape=...]
    unnamed x9 -> x1, local copies, waits for them, and re-layouts: 5.2 us -> 1.67 us
where the time goes in v2:
time: 60.3 us; the launch traced here: 59.7 us
  Pallas kernels  57.4 us (95%)
  local copies, waits for them, and re-layouts  1.67 us (3%)
  between operations  0.66 us (1%)
    pallas_call x1, Pallas kernels, per_device(): pl.pallas_call(functools.partial(kernel, nchain, nseg, depth), out_shape=...  57.4 us
    unnamed x1, local copies, waits for them, and re-layouts  1.67 us

profile of v2, /device:TPU:9, one launch (start us, length us, event | category | flops | bytes accessed | tf_op | source)
XLA Modules:
  0.0 59.7 jit_solution(9307452256686893034)
XLA Ops:
  0.7 57.4 %shard_map.55 = f32[256,256]{1,0:T(8,128)} custom-call(bf16[7,1024,256]{2,1,0:T(8,128)(2,1)} %bitcast.5, s32[1]{0:T(128)S(6)} %copy.7.widths, f32[256,256]{1,0:T(8,128)} %warm.1, f32[64,256]{1,0:T(8,128)} %bitcast.6, f32[1,256]{1,0:T(1,128)} %bitcast.7), custom_call_target="tpu_custom_call" | custom-call | tf_op jit(solution)/shard_map/pallas_call | solution.py:344
  58.0 1.7 %copy.8 = f32[256,256]{1,0:T(8,128)} copy(f32[256,256]{1,0:T(8,128)} %shard_map.55) | data formatting | bytes 524288

commit v3 on v2

--- a/solution.py
+++ b/solution.py
@@ -31,8 +31,12 @@
     above = {"chain": chain + 2, "seg": seg}
     has_below, has_above = p >= 1, p + 1 < pairs
 
+    def facing(o):
+        flip = seg if o < 2 else seg + 2 - 4 * (seg // 2)
+        return flip + 1 - 2 * (seg % 2) if o % 2 else flip
+
     def peer(o):
-        return {"chain": chain, "seg": lax.rem(seg + o, nseg)}
+        return {"chain": chain, "seg": facing(o)}
 
     def loads(j):
         return pltpu.make_async_copy(tiles_hbm.at[j], tiles.at[j], tile_sem.at[j])
@@ -94,7 +98,8 @@
 
     def transfers(it):
         def ag_copy(o):
-            return send(cur_t.at[it], ag.at[it, o - 1], ag_s.at[it, o - 1], ag_r.at[it, o - 1], peer(o))
+            src = ag.at[it, 1] if o == 3 else cur_t.at[it]
+            return send(src, ag.at[it, o - 1], ag_s.at[it, o - 1], ag_r.at[it, o - 1], peer(o % 2 or 2))
 
         def even_copy(d):
             src = cur.at[it] if d == 0 else even.at[it, d]
@@ -119,7 +124,7 @@
             return send(q_send.at[it], q_recv.at[it], q_s.at[it], q_r.at[it], partner)
 
         def rs_copy(o):
-            return send(rs_send.at[it, o - 1], rs_recv.at[it, o - 1], rs_s.at[it, o - 1], rs_r.at[it, o - 1], peer(o))
+            return send(rs_send.at[it, o - 1], rs_recv.at[it, o - 1], rs_s.at[it, o - 1], rs_r.at[it, o - 1], peer(o % 2 or 2))
 
         return ag_copy, even_copy, odd_copy, cross_copy, up_copy, y_copy, q_copy, rs_copy
 
@@ -130,7 +135,7 @@
         pl.when(has_below)(lambda: even_copy(0).start())
         pl.when(y == 1)(lambda: cross_copy(0).start())
         cur_t[it] = now.T.astype(BF16)
-        for o in range(1, nseg):
+        for o in (2, 1):
             ag_copy(o).start()
 
         yield
@@ -148,15 +153,17 @@
             pl.when(has_below)(lambda: even_copy(1).start())
             cross_copy(1).start()
 
-        for o in range(1, nseg):
-            ag_copy(o).wait_recv()
+        ag_copy(2).wait_recv()
+        ag_copy(3).start()
+        ag_copy(1).wait_recv()
+        ag_copy(3).wait_recv()
 
         def product(j):
             total = jnp.dot(
                 cur_t[it], tiles[j, pl.ds(pl.multiple_of(seg * strip, strip), strip), :], preferred_element_type=F32
             )
             for o in range(1, nseg):
-                owner = lax.rem(seg - o + nseg, nseg)
+                owner = facing(o)
                 rows = pl.ds(pl.multiple_of(owner * strip, strip), strip)
                 total = total + jnp.dot(ag[it, o - 1], tiles[j, rows, :], preferred_element_type=F32)
             return total * live(j)
@@ -264,9 +271,13 @@
                 total = total + term(rows, j)
             return total
 
-        for o in range(1, nseg):
-            rs_send[it, o - 1] = rest(lax.rem(seg + o, nseg)).astype(BF16)
+        for o in (3, 1):
+            rs_send[it, o - 1] = rest(facing(o)).astype(BF16)
             rs_copy(o).start()
+        across = rest(facing(2))
+        rs_copy(3).wait_recv()
+        rs_send[it, 1] = (across + rs_recv[it, 2].astype(F32)).astype(BF16)
+        rs_copy(2).start()
         forward = rest(seg)
         yield
         back = product(0)
@@ -274,7 +285,7 @@
         pl.when(y == 1)(lambda: q_copy().wait_recv())
         back = back + b_recv[it, 0, 0].astype(F32) + q_recv[it].astype(F32)
         coupled = forward + back.T
-        for o in range(1, nseg):
+        for o in (1, 2):
             rs_copy(o).wait_recv()
             coupled = coupled + rs_recv[it, o - 1].astype(F32)
         now = est[:, columns]

time: 60.3 us -> 59.5 us (0.987)
  no operation moved by 1% of the time
where the time goes in v3:
time: 59.5 us; the launch traced here: 59.2 us
  Pallas kernels  56.8 us (95%)
  local copies, waits for them, and re-layouts  1.67 us (3%)
  between operations  0.66 us (1%)
    pallas_call x1, Pallas kernels, per_device(): pl.pallas_call(functools.partial(kernel, nchain, nseg, depth), out_shape=...  56.8 us
    unnamed x1, local copies, waits for them, and re-layouts  1.67 us

profile of v3, /device:TPU:9, one launch (start us, length us, event | category | flops | bytes accessed | tf_op | source)
XLA Modules:
  0.0 59.2 jit_solution(7368007316100488085)
XLA Ops:
  0.7 56.8 %shard_map.55 = f32[256,256]{1,0:T(8,128)} custom-call(bf16[7,1024,256]{2,1,0:T(8,128)(2,1)} %bitcast.5, s32[1]{0:T(128)S(6)} %copy.7.widths, f32[256,256]{1,0:T(8,128)} %warm.1, f32[64,256]{1,0:T(8,128)} %bitcast.6, f32[1,256]{1,0:T(1,128)} %bitcast.7), custom_call_target="tpu_custom_call" | custom-call | tf_op jit(solution)/shard_map/pallas_call | solution.py:355
  57.5 1.7 %copy.8 = f32[256,256]{1,0:T(8,128)} copy(f32[256,256]{1,0:T(8,128)} %shard_map.55) | data formatting | bytes 524288
